TPU v7x, 32 devices: a whole 2x2x4 slice. The times are simulated.
32 devices in a mesh: parts: 2 (over x), fibre: 16 (over z, y, core).
Axes of the slice: x: 2, y: 2, z: 4, core: 2. Of those that a mesh axis runs over, the one named last changes fastest.
Arguments:
- signal: bfloat16 [64, 16, 8192], P('parts', None, 'fibre'), parts along dimension 0, may hold values from -6 to 6
- conv_taps: bfloat16 [5, 5, 64, 32], replicated, may hold values from -0.21875 to 0.21875
- response: float32 [2, 64, 4096], P(None, 'fibre'), may hold values from -4 to 4
- cotangent: bfloat16 [128, 8, 4096], P('parts', None, 'fibre'), parts along dimension 0, may hold values from -6 to 6
Outputs:
- input_grad: bfloat16 [64, 16, 8192], P('parts', None, 'fibre'), parts along dimension 0
- tap_grad: float32 [10, 5, 64, 32], P('parts'), parts along dimension 0
- filter_grad: float32 [4, 64, 4096], P('parts', 'fibre'), parts along dimension 0
There are 2 independent parts, one for each index of `parts`. A program takes and returns all parts, laid end to end along the dimension named above; an argument that names none is the same for every part. Nothing has to cross between parts.
All inputs are finite; a program needn't handle non-finite values.
Results may differ from a plain program's by a relative error of at most 0.012.
Values may be sent and summed in bfloat16 or wider, within the bound.
A program may use at most 64 MiB of HBM per device.

v0:
```python
import math

import jax
import jax.numpy as jnp
import numpy as np
from jax import lax
from jax.experimental import pallas as pl
from jax.experimental.pallas import tpu as pltpu
from jax.sharding import PartitionSpec as P

inv_root_two = 1.0 / math.sqrt(2.0)
inv_root_tau = 1.0 / math.sqrt(2.0 * math.pi)
lanes = 128
f32 = jnp.float32
bf16 = jnp.bfloat16
vmem_bytes = 50 * 1024 * 1024


def log2(size):
    bits = size.bit_length() - 1
    assert 1 << bits == size
    return bits


def dot(left, right):
    return jnp.dot(left, right, preferred_element_type=f32)


def one_hot(rows, cols, wanted):
    axis = 0 if wanted.shape[0] == 1 else 1
    index = lax.broadcasted_iota(jnp.int32, (rows, cols), axis)
    return jnp.where(index == wanted, 1.0, 0.0).astype(bf16)


def swap_rows(outer, inner):
    count = outer * inner
    row = lax.broadcasted_iota(jnp.int32, (count, 1), 0)
    source = (row & (inner - 1)) * outer + (row >> log2(inner))
    return one_hot(count, count, source)


def conv_kernel(cin, tw, ks, cout, th, x_ref, w_ref, pp_ref, out_ref, ct_ref):
    width = x_ref.shape[1] - lanes
    half = width // 2
    x2 = dot(swap_rows(tw, cin), x_ref[...]).astype(bf16)
    blank = jnp.zeros((2 * ks * cin, half), bf16)
    pp_ref[0 : 2 * ks * cin, :] = blank
    pp_ref[(tw + 2) * ks * cin : (tw + 4) * ks * cin, :] = blank
    for j in range(ks):
        m = 2 * lax.broadcasted_iota(jnp.int32, (1, half), 1) + (j - 2)
        source = jnp.where(m < 0, width + 2 + m, jnp.where(m >= width, m + 2, m))
        pj = dot(x2, one_hot(width + lanes, half, source)).astype(bf16)
        for s in range(tw):
            at = ((s + 2) * ks + j) * cin
            pp_ref[at : at + cin, :] = pj[s * cin : (s + 1) * cin, :]
    step = 2 * ks * cin
    for t in range(th):
        patches = pp_ref[t * step : t * step + ks * ks * cin, :]
        ct_ref[t * cout : (t + 1) * cout, :] = dot(w_ref[...], patches).astype(bf16)
    out_ref[...] = dot(swap_rows(cout, th), ct_ref[...]).astype(bf16)


def split(values):
    high = values.astype(bf16)
    return high, (values - high.astype(f32)).astype(bf16)


def dot_split(left, right):
    return dot(left[0], right[0]) + (dot(left[0], right[1]) + dot(left[1], right[0]))


def filter_kernel(
    chans, th, rv_ref, re_ref, im_ref, o1_ref, o1b_ref, i2_ref, i2b_ref, tc_ref, ts_ref, fg_ref, out_ref
):
    blocks = rv_ref.shape[0]
    per = rv_ref.shape[2] // lanes
    outer = blocks * per
    rows = outer * th
    waves = outer * lanes
    o1 = (o1_ref[0], o1_ref[1])
    o1b = (o1b_ref[0], o1b_ref[1])
    i2 = (i2_ref[0], i2_ref[1])
    i2b = (i2b_ref[0], i2b_ref[1])
    tcos = tc_ref[...]
    tsin = ts_ref[...]

    def gathered(first):
        cols = []
        whole = [rv_ref[d].astype(f32) for d in range(blocks)]
        for c in range(chans):
            tiles = []
            for d in range(blocks):
                at = first + c * th
                for h in range(per):
                    tiles.append(whole[d][at : at + th, h * lanes : (h + 1) * lanes])
            cols.append(jnp.concatenate(tiles, axis=0))
        return jnp.concatenate(cols, axis=1)

    def forward(first):
        wide = []
        for c in range(chans):
            fr = first[:rows, c * lanes : (c + 1) * lanes]
            fi = first[rows:, c * lanes : (c + 1) * lanes]
            wide.append(jnp.concatenate([fr * tcos + fi * tsin, fi * tcos - fr * tsin], axis=1))
        spec = dot_split(split(jnp.concatenate(wide, axis=0)), i2)
        return spec[:, :lanes], spec[:, lanes:]

    def backward(sr, si):
        back = dot_split(split(jnp.concatenate([sr, si], axis=1)), i2b)
        cols = []
        for c in range(chans):
            br = back[c * rows : (c + 1) * rows, :lanes]
            bi = back[c * rows : (c + 1) * rows, lanes:]
            cols.append(jnp.concatenate([br * tcos - bi * tsin, bi * tcos + br * tsin], axis=0))
        return dot_split(o1b, split(jnp.concatenate(cols, axis=1))) * (1.0 / waves)

    def spread(ref):
        flat = ref[...]
        return jnp.broadcast_to(flat[:, None, :], (flat.shape[0], th, lanes)).reshape(
            flat.shape[0] * th, lanes
        )

    resp_r = spread(re_ref)
    resp_i = spread(im_ref)
    x = gathered(0).astype(bf16)
    sr, si = forward(dot(o1[0], x) + dot(o1[1], x))
    v = backward(resp_r * sr - resp_i * si, resp_r * si + resp_i * sr)
    slope = 0.5 * (1.0 + lax.erf(v * inv_root_two)) + v * jnp.exp(-0.5 * v * v) * inv_root_tau
    g = gathered(chans * th) * slope
    gr, gi = forward(dot_split(o1, split(g)))
    scale = 1.0 / waves
    fg_ref[0] = jnp.sum((sr * gr + si * gi).reshape(chans * outer, th, lanes), axis=1) * scale
    fg_ref[1] = jnp.sum((sr * gi - si * gr).reshape(chans * outer, th, lanes), axis=1) * scale
    y = backward(resp_r * gr + resp_i * gi, resp_r * gi - resp_i * gr)
    lane = lax.broadcasted_iota(jnp.int32, (th, lanes), 1)
    zero = jnp.zeros((th, lanes), f32)
    for d in range(blocks):
        parts = []
        for c in range(chans):
            col = y[:, c * lanes : (c + 1) * lanes]
            low = col[(d * per - 1) * th : d * per * th] if d > 0 else zero
            high = col[(d + 1) * per * th : ((d + 1) * per + 1) * th] if d < blocks - 1 else zero
            rim = jnp.where(lane == lanes - 1, low, jnp.where(lane == 0, high, 0.0))
            tiles = [col[(d * per + h) * th : (d * per + h + 1) * th] for h in range(per)]
            parts.append(jnp.concatenate(tiles + [rim], axis=1))
        out_ref[d] = jnp.concatenate(parts, axis=0).astype(bf16)


def taps_kernel(cin, ks, cout, th, g_ref, pp_ref, gt_ref, tap_ref):
    half = pp_ref.shape[1]
    gt_ref[...] = dot(swap_rows(th, cout), g_ref[...]).astype(bf16)
    step = 2 * ks * cin
    total = None
    for t in range(th):
        term = lax.dot_general(
            gt_ref[t * cout : (t + 1) * cout, :half],
            pp_ref[t * step : t * step + ks * ks * cin, :],
            (((1,), (1,)), ((), ())),
            preferred_element_type=f32,
        )
        total = term if total is None else total + term
    tap_ref[...] = total


def input_kernel(cin, tw, cout, th, gt_ref, v_ref, out_ref, gg_ref, xo_ref):
    ext = gt_ref.shape[1]
    half = ext - lanes
    blank = jnp.zeros((3 * cout, half), bf16)
    gg_ref[0 : 3 * cout, :] = blank
    gg_ref[(th + 1) * 3 * cout : (th + 2) * 3 * cout, :] = blank
    p = lax.broadcasted_iota(jnp.int32, (1, half), 1)
    g2 = gt_ref[...]
    for sh in range(3):
        if sh == 1:
            moved = g2[:, :half]
        else:
            source = p + 1 if sh == 0 else jnp.where(p == 0, ext - 1, p - 1)
            moved = dot(g2, one_hot(ext, half, source)).astype(bf16)
        for t in range(th):
            at = ((t + 1) * 3 + sh) * cout
            gg_ref[at : at + cout, :] = moved[t * cout : (t + 1) * cout, :]
    for q in range(th):
        dx = dot(v_ref[...], gg_ref[q * 3 * cout : (q + 3) * 3 * cout, :]).astype(bf16)
        for ps in range(2):
            for pm in range(2):
                at = (ps * 2 + pm) * cin
                row = (2 * q + ps) * cin
                xo_ref[row : row + cin, pm * half : (pm + 1) * half] = dx[at : at + cin, :]
    m = lax.broadcasted_iota(jnp.int32, (1, 2 * half), 1)
    weave = one_hot(2 * half, 2 * half, (m & 1) * half + (m >> 1))
    woven = dot(xo_ref[...], weave).astype(bf16)
    out_ref[...] = dot(swap_rows(cin, tw), woven).astype(bf16)


def dft_tables(outer, th):
    waves = outer * lanes
    turn = 2.0 * math.pi
    a = np.arange(outer)
    b = np.arange(lanes)
    ang = turn * ((a[:, None] * a[None, :]) % outer) / outer
    eye = np.eye(th)
    o1 = np.concatenate([np.kron(np.cos(ang), eye), -np.kron(np.sin(ang), eye)], axis=0)
    ang = turn * ((b[:, None] * b[None, :]) % lanes) / lanes
    i2 = np.block([[np.cos(ang), -np.sin(ang)], [np.sin(ang), np.cos(ang)]])
    ang = np.repeat(turn * (a[:, None] * b[None, :]) / waves, th, axis=0)

    def halves(table):
        table = table.astype(np.float32)
        high = table.astype(bf16)
        return np.stack([high, (table - high.astype(np.float32)).astype(bf16)])

    return (
        halves(o1),
        halves(o1.T),
        halves(i2),
        halves(i2.T),
        np.cos(ang).astype(np.float32),
        np.sin(ang).astype(np.float32),
    )


def call(body, out_shape, scratch=(), flops=0):
    many = isinstance(out_shape, (list, tuple))
    return pl.pallas_call(
        body,
        out_shape=out_shape,
        out_specs=[pl.BlockSpec(memory_space=pltpu.VMEM)] * len(out_shape)
        if many
        else pl.BlockSpec(memory_space=pltpu.VMEM),
        scratch_shapes=list(scratch),
        compiler_params=pltpu.CompilerParams(vmem_limit_bytes=vmem_bytes),
        cost_estimate=pl.CostEstimate(flops=flops, bytes_accessed=4000000, transcendentals=0),
    )


def phase_weights(conv_taps):
    ks, _, cout, cin = conv_taps.shape
    none = jnp.zeros((cin, cout), conv_taps.dtype)
    turned = conv_taps.transpose(0, 1, 3, 2)
    rows = []
    for ps in range(2):
        for pm in range(2):
            cols = []
            for ti in range(3):
                i = 4 - 2 * ti + ps
                for sh in range(3):
                    j = 2 * sh + pm
                    if ps:
                        i = (None, 3, 1)[ti]
                    inside = i is not None and i < ks and j < ks
                    cols.append(turned[i, j] if inside else none)
            rows.append(jnp.concatenate(cols, axis=1))
    return jnp.concatenate(rows, axis=0)


def per_device(signal, conv_taps, response, cotangent):
    ks, _, cout, cin = conv_taps.shape
    tw, width = signal.shape[1:]
    th, half = cotangent.shape[1:]
    count = lax.axis_size("fibre")
    chans = response.shape[1]
    waves = response.shape[2]
    outer = waves // lanes
    shape = jax.ShapeDtypeStruct

    up = [(i, i + 1) for i in range(count - 1)]
    down = [(b, a) for a, b in up]
    low = lax.ppermute(signal[:, :, width - 2 :], "fibre", up)
    high = lax.ppermute(signal[:, :, :2], "fibre", down)
    rim = jnp.pad(jnp.concatenate([low, high], axis=2), ((0, 0), (0, 0), (0, lanes - 4)))
    ext = jnp.concatenate([signal, rim], axis=2).reshape(cin * tw, width + lanes)
    taps_flat = conv_taps.transpose(2, 0, 1, 3).reshape(cout, ks * ks * cin)
    weights = phase_weights(conv_taps)
    tables = dft_tables(outer, th)
    arranged = response.reshape(2, chans, lanes, outer).transpose(0, 1, 3, 2)
    arranged = arranged.reshape(2, chans * outer, lanes)

    def conv_body(*refs):
        conv_kernel(cin, tw, ks, cout, th, *refs)

    patches, conv_out = call(
        conv_body,
        [shape(((tw + 4) * ks * cin, half), bf16), shape((cout * th, half), bf16)],
        [pltpu.VMEM((cout * th, half), bf16)],
    )(ext, taps_flat)

    group = chans * th
    sent = jnp.concatenate(
        [conv_out.reshape(count, group, half), cotangent.reshape(count, group, half)], axis=1
    )
    got = lax.all_to_all(sent, "fibre", split_axis=0, concat_axis=0, tiled=True)

    def filter_body(*refs):
        filter_kernel(chans, th, *refs)

    fgrad, blocks = call(
        filter_body,
        [shape((2, chans * outer, lanes), f32), shape((count, group, half + lanes), bf16)],
    )(got, arranged[0], arranged[1], *tables)
    filter_grad = (
        fgrad.reshape(2, chans, outer, lanes).transpose(0, 1, 3, 2).reshape(2, chans, waves)
    )
    grads = lax.all_to_all(blocks, "fibre", split_axis=0, concat_axis=0, tiled=True)
    grads = grads.reshape(cout * th, half + lanes)

    def taps_body(*refs):
        taps_kernel(cin, ks, cout, th, *refs)

    turned, local_taps = call(
        taps_body,
        [shape((cout * th, half + lanes), bf16), shape((cout, ks * ks * cin), f32)],
    )(grads, patches)
    share = cout * ks * ks * cin // count
    terms = lax.all_to_all(
        local_taps.reshape(count, 8, share // 8), "fibre", split_axis=0, concat_axis=0, tiled=True
    )

    def input_body(*refs):
        input_kernel(cin, tw, cout, th, *refs)

    input_grad = call(
        input_body,
        shape((cin * tw, width), bf16),
        [pltpu.VMEM(((th + 2) * 3 * cout, half), bf16), pltpu.VMEM((cin * tw, width), bf16)],
        flops=1500000000,
    )(turned, weights)

    part = jnp.sum(terms, axis=0) * (1.0 / math.sqrt(th * waves))
    all_taps = lax.all_to_all(
        jnp.broadcast_to(part[None], (count, 8, share // 8)),
        "fibre",
        split_axis=0,
        concat_axis=0,
        tiled=True,
    )
    tap_grad = all_taps.reshape(cout, ks, ks, cin).transpose(1, 2, 0, 3)
    return (input_grad.reshape(signal.shape), tap_grad, filter_grad)


def solution(mesh):
    in_specs = (P("parts", None, "fibre"), P(), P(None, "fibre", None), P("parts", None, "fibre"))
    out_specs = (P("parts", None, "fibre"), P("parts", None, None, None), P("parts", "fibre", None))
    return jax.shard_map(
        per_device, mesh=mesh, in_specs=in_specs, out_specs=out_specs, check_vma=False
    )
```

profile of v0, /device:TPU:0, one launch (start us, length us, event | category | flops | bytes accessed | tf_op | source)
XLA Modules:
  0.0 93.0 jit_solution(10525413922807314551)
XLA Ops:
  0.6 1.1 %fusion.3 = (bf16[32,16,2]{2,1,0:T(8,128)(2,1)S(1)}, bf16[32,16,2]{2,1,0:T(8,128)(2,1)S(1)}) fusion(bf16[32,16,512]{2,1,0:T(8,128)(2,1)} %param.10), kind=kLoop, calls=%fused_computation.33 | loop fusion | bytes 8192 | tf_op jit(solution)/shard_map/slice | solution.py:268
  1.8 0.2 copy.30
  2.0 1.3 %collective-permute-start.1 = (bf16[32,16,2]{0,1,2:T(8,128)(2,1)S(1)}, bf16[32,16,2]{0,1,2:T(8,128)(2,1)S(1)}, u32[]{:S(2)}, u32[]{:S(2)}) collective-permute-start(bf16[32,16,2]{0,1,2:T(8,128)(2,1)S(1)} %copy.30), channel_id=1, source_target_pairs={{1,0},{2,1},{3,2},{4,3},{5,4},{6,5},{7,6},{8,7},{9,8},{10,9},{11,1... | collective-permute-start | bytes 6152 | tf_op jit(solution)/shard_map/ppermute | solution.py:269
  3.3 0.2 copy.29
  3.5 3.2 %collective-permute-start = (bf16[32,16,2]{0,1,2:T(8,128)(2,1)S(1)}, bf16[32,16,2]{0,1,2:T(8,128)(2,1)S(1)}, u32[]{:S(2)}, u32[]{:S(2)}) collective-permute-start(bf16[32,16,2]{0,1,2:T(8,128)(2,1)S(1)} %copy.29), channel_id=1, source_target_pairs={{0,1},{1,2},{2,3},{3,4},{4,5},{5,6},{6,7},{7,8},{8,9},{9,10},{10,1... | collective-permute-start | bytes 6152 | tf_op jit(solution)/shard_map/ppermute | solution.py:268
  6.6 1.1 %copy.24.refs_1_ = bf16[64,800]{1,0:T(8,128)(2,1)S(1)} copy(bf16[64,800]{0,1:T(8,128)(2,1)} %bitcast.76) | data formatting | bytes 204800 | tf_op jit(solution)/shard_map/reshape | solution.py:272
  8.0 2.6 %shard_map.121 = (bf16[3200,256]{1,0:T(8,128)(2,1)S(1)}, bf16[512,256]{1,0:T(8,128)(2,1)S(1)}) custom-call(bf16[512,640]{1,0:T(8,128)(2,1)S(1)} %bitcast.67, bf16[64,800]{1,0:T(8,128)(2,1)S(1)} %copy.24.refs_1_), custom_call_target="tpu_custom_call" | custom-call | bytes 4000000 | tf_op jit(solution)/shard_map/pallas_call | solution.py:281
  10.7 0.8 pad_maximum_fusion
  11.5 9.6 %all-to-all-start = ((bf16[16,64,256]{2,1,0:T(8,128)(2,1)}), bf16[16,64,256]{2,1,0:T(8,128)(2,1)S(1)}, u32[]{:S(2)}, u32[]{:S(2)}) async-start(bf16[16,64,256]{2,1,0:T(8,128)(2,1)} %pad_maximum_fusion), calls=%async_computation | async-start | bytes 1048576 | tf_op jit(solution)/shard_map/all_to_all | solution.py:291
  21.2 2.0 %reshape.51 = f32[2,4,128,32]{3,2,1,0:T(8,128)} reshape(f32[2,4,4096]{2,1,0:T(4,128)} %param.12) | data formatting | bytes 262144 | tf_op jit(solution)/shard_map/reshape | solution.py:275
  23.2 1.9 %fusion.2 = (f32[1,4,32,128]{2,3,1,0:T(8,128)}, f32[1,4,32,128]{2,3,1,0:T(8,128)}) fusion(f32[2,4,32,128]{2,3,1,0:T(8,128)} %bitcast.75), kind=kLoop, calls=%fused_computation.32 | loop fusion | bytes 262144 | tf_op jit(solution)/shard_map/slice | solution.py:299
  25.1 1.0 %copy.26 = f32[1,4,32,128]{3,2,1,0:T(8,128)S(1)} copy(f32[1,4,32,128]{2,3,1,0:T(8,128)} %get-tuple-element.21) | data formatting | bytes 131072 | tf_op jit(solution)/shard_map/slice | solution.py:299
  26.1 1.7 %copy.25 = f32[1,4,32,128]{3,2,1,0:T(8,128)} copy(f32[1,4,32,128]{2,3,1,0:T(8,128)} %get-tuple-element.22) | data formatting | bytes 131072 | tf_op jit(solution)/shard_map/slice | solution.py:299
  27.8 7.8 %all-to-all-done.refs_0_ = bf16[16,64,256]{2,1,0:T(8,128)(2,1)S(1)} async-done(((bf16[16,64,256]{2,1,0:T(8,128)(2,1)}), bf16[16,64,256]{2,1,0:T(8,128)(2,1)S(1)}, u32[]{:S(2)}, u32[]{:S(2)}) %all-to-all-start) | async-done | bytes 524320 | tf_op jit(solution)/shard_map/all_to_all | solution.py:291
  35.7 0.9 %copy-done.3 = bf16[2,256,256]{2,1,0:T(8,128)(2,1)S(1)} copy-done((bf16[2,256,256]{2,1,0:T(8,128)(2,1)S(1)}, bf16[2,256,256]{2,1,0:T(8,128)(2,1)}, u32[]{:S(2)}) %copy-start.3) | copy-done | bytes 262168
  36.6 0.8 copy-done.4
  37.4 0.9 copy-done.7
  38.3 0.9 copy-done.8
  39.2 5.5 %shard_map.122 = (f32[2,128,128]{2,1,0:T(8,128)S(1)}, bf16[16,32,384]{2,1,0:T(8,128)(2,1)S(1)}) custom-call(bf16[16,64,256]{2,1,0:T(8,128)(2,1)S(1)} %all-to-all-done.refs_0_, f32[128,128]{1,0:T(8,128)S(1)} %bitcast.70, f32[128,128]{1,0:T(8,128)S(1)} %bitcast.69, bf16[2,512,256]{2,1,0:T(8,128)(2,1)S(1)} %copy-done.1, bf16[2,256,512]{2,1,0:T(8,128)(2,1)S(1)} %copy-done, ...), custom_call_target="tpu_custom_call" | custom-call | bytes 4000000 | tf_op jit(solution)/shard_map/pallas_call | solution.py:296
  44.7 0.6 copy-done.5
  45.4 16.1 %all_to_all.20 = bf16[16,32,384]{2,1,0:T(8,128)(2,1)S(1)} all-to-all(bf16[16,32,384]{2,1,0:T(8,128)(2,1)S(1)} %get-tuple-element.10), channel_id=1, replica_groups=mesh['parts'=2,'fibre'=16] {'fibre'}, dimensions={0} | all-to-all | bytes 786432 | tf_op jit(solution)/shard_map/all_to_all | solution.py:303
  61.5 1.4 %shard_map.123 = (bf16[512,384]{1,0:T(8,128)(2,1)S(1)}, f32[64,800]{1,0:T(8,128)S(1)}) custom-call(bf16[512,384]{1,0:T(8,128)(2,1)S(1)} %bitcast.68, bf16[3200,256]{1,0:T(8,128)(2,1)S(1)} %get-tuple-element.11.refs_1_), custom_call_target="tpu_custom_call" | custom-call | bytes 4000000 | tf_op jit(solution)/shard_map/pallas_call | solution.py:309
  62.9 0.8 reshape.54
  63.7 3.5 %all-to-all-start.2 = ((f32[16,8,400]{2,1,0:T(8,128)}), f32[16,8,400]{2,1,0:T(8,128)S(1)}, u32[]{:S(2)}, u32[]{:S(2)}) async-start(f32[16,8,400]{2,1,0:T(8,128)} %reshape.54), calls=%async_computation.2 | async-start | bytes 524288 | tf_op jit(solution)/shard_map/all_to_all | solution.py:314
  67.6 9.7 %all-to-all-done.2 = f32[16,8,400]{2,1,0:T(8,128)S(1)} async-done(((f32[16,8,400]{2,1,0:T(8,128)}), f32[16,8,400]{2,1,0:T(8,128)S(1)}, u32[]{:S(2)}, u32[]{:S(2)}) %all-to-all-start.2) | async-done | bytes 204832 | tf_op jit(solution)/shard_map/all_to_all | solution.py:314
  77.3 0.7 broadcast_in_dim.10
  78.0 3.5 %all-to-all-start.3 = ((f32[16,8,400]{2,1,0:T(8,128)}), f32[16,8,400]{2,1,0:T(8,128)S(1)}, u32[]{:S(2)}, u32[]{:S(2)}) async-start(f32[16,8,400]{2,1,0:T(8,128)} %broadcast_in_dim.10), calls=%async_computation.3 | async-start | bytes 524288 | tf_op jit(solution)/shard_map/all_to_all | solution.py:329
  81.9 0.9 reshape.57
  82.8 2.3 %shard_map.124 = bf16[512,512]{1,0:T(8,128)(2,1)} custom-call(bf16[512,384]{1,0:T(8,128)(2,1)S(1)} %get-tuple-element.12.refs_0_, bf16[128,576]{1,0:T(8,128)(2,1)S(1)} %pad_maximum_fusion.1.refs_1_), custom_call_target="tpu_custom_call" | custom-call | flops 1500000000 | bytes 4000000 | tf_op jit(solution)/shard_map/pallas_call | solution.py:321
  85.1 6.4 %all-to-all-done.3 = f32[16,8,400]{2,1,0:T(8,128)S(1)} async-done(((f32[16,8,400]{2,1,0:T(8,128)}), f32[16,8,400]{2,1,0:T(8,128)S(1)}, u32[]{:S(2)}, u32[]{:S(2)}) %all-to-all-start.3) | async-done | bytes 204832 | tf_op jit(solution)/shard_map/all_to_all | solution.py:329
  91.6 0.4 reshape.55
  92.0 1.1 %copy.28 = f32[5,5,64,32]{2,3,1,0:T(8,128)} copy(f32[5,5,64,32]{3,1,0,2:T(8,128)S(1)} %bitcast.73) | data formatting | bytes 409600
  (36 shorter events, 1.0 us)
Async XLA Ops:
  0.6 7.3 %copy-start.9 = (bf16[32,16,512]{2,1,0:T(8,128)(2,1)S(1)}, bf16[32,16,512]{2,1,0:T(8,128)(2,1)}, u32[]{:S(2)}) copy-start(bf16[32,16,512]{2,1,0:T(8,128)(2,1)} %param.10) | copy-start | bytes 1572868
  2.0 5.7 %collective-permute-start.1 = (bf16[32,16,2]{0,1,2:T(8,128)(2,1)S(1)}, bf16[32,16,2]{0,1,2:T(8,128)(2,1)S(1)}, u32[]{:S(2)}, u32[]{:S(2)}) collective-permute-start(bf16[32,16,2]{0,1,2:T(8,128)(2,1)S(1)} %copy.30), channel_id=1, source_target_pairs={{1,0},{2,1},{3,2},{4,3},{5,4},{6,5},{7,6},{8,7},{9,8},{10,9},{11,1... | collective-permute-start | bytes 6152 | tf_op jit(solution)/shard_map/ppermute | solution.py:269
  3.5 7.2 %copy-start.11 = (bf16[64,8,256]{2,1,0:T(8,128)(2,1)S(1)}, bf16[64,8,256]{2,1,0:T(8,128)(2,1)}, u32[]{:S(2)}) copy-start(bf16[64,8,256]{2,1,0:T(8,128)(2,1)} %param.13) | copy-start | bytes 786436
  3.5 4.2 %collective-permute-start = (bf16[32,16,2]{0,1,2:T(8,128)(2,1)S(1)}, bf16[32,16,2]{0,1,2:T(8,128)(2,1)S(1)}, u32[]{:S(2)}, u32[]{:S(2)}) collective-permute-start(bf16[32,16,2]{0,1,2:T(8,128)(2,1)S(1)} %copy.29), channel_id=1, source_target_pairs={{0,1},{1,2},{2,3},{3,4},{4,5},{5,6},{6,7},{7,8},{8,9},{9,10},{10,1... | collective-permute-start | bytes 6152 | tf_op jit(solution)/shard_map/ppermute | solution.py:268
  11.5 24.1 %all-to-all-start = ((bf16[16,64,256]{2,1,0:T(8,128)(2,1)}), bf16[16,64,256]{2,1,0:T(8,128)(2,1)S(1)}, u32[]{:S(2)}, u32[]{:S(2)}) async-start(bf16[16,64,256]{2,1,0:T(8,128)(2,1)} %pad_maximum_fusion), calls=%async_computation | async-start | bytes 1048576 | tf_op jit(solution)/shard_map/all_to_all | solution.py:291
  21.2 14.5 %copy-start = (bf16[2,256,512]{2,1,0:T(8,128)(2,1)S(1)}, bf16[2,256,512]{2,1,0:T(8,128)(2,1)}, u32[]{:S(2)}) copy-start(bf16[2,256,512]{2,1,0:T(8,128)(2,1)} %constant.22.clone.refs_4_) | copy-start | bytes 1572868
  21.2 14.5 %copy-start.1 = (bf16[2,512,256]{2,1,0:T(8,128)(2,1)S(1)}, bf16[2,512,256]{2,1,0:T(8,128)(2,1)}, u32[]{:S(2)}) copy-start(bf16[2,512,256]{2,1,0:T(8,128)(2,1)} %constant.8.clone.refs_3_) | copy-start | bytes 1572868
  21.2 14.4 %copy-start.2 = (bf16[2,256,256]{2,1,0:T(8,128)(2,1)S(1)}, bf16[2,256,256]{2,1,0:T(8,128)(2,1)}, u32[]{:S(2)}) copy-start(bf16[2,256,256]{2,1,0:T(8,128)(2,1)} %constant.24.clone.refs_6_) | copy-start | bytes 786436
  35.6 1.0 %copy-start.3 = (bf16[2,256,256]{2,1,0:T(8,128)(2,1)S(1)}, bf16[2,256,256]{2,1,0:T(8,128)(2,1)}, u32[]{:S(2)}) copy-start(bf16[2,256,256]{2,1,0:T(8,128)(2,1)} %constant.23.clone.refs_5_) | copy-start | bytes 786436
  36.6 0.8 copy-start.4
  37.4 0.9 copy-start.7
  38.3 0.9 copy-start.8
  44.7 0.7 copy-start.5
  61.5 5.8 %copy-start.10 = (bf16[5,5,64,32]{2,3,1,0:T(8,128)(2,1)S(1)}, bf16[5,5,64,32]{2,3,1,0:T(8,128)(2,1)}, u32[]{:S(2)}) copy-start(bf16[5,5,64,32]{2,3,1,0:T(8,128)(2,1)} %param.11) | copy-start | bytes 307204
  63.7 13.6 %all-to-all-start.2 = ((f32[16,8,400]{2,1,0:T(8,128)}), f32[16,8,400]{2,1,0:T(8,128)S(1)}, u32[]{:S(2)}, u32[]{:S(2)}) async-start(f32[16,8,400]{2,1,0:T(8,128)} %reshape.54), calls=%async_computation.2 | async-start | bytes 524288 | tf_op jit(solution)/shard_map/all_to_all | solution.py:314
  67.2 14.5 %copy-start.6 = (f32[2,128,128]{2,1,0:T(8,128)S(1)}, f32[2,128,128]{2,1,0:T(8,128)}, u32[]{:S(2)}) copy-start(f32[2,128,128]{2,1,0:T(8,128)} %copy-done.5) | copy-start | bytes 393220
  78.0 13.5 %all-to-all-start.3 = ((f32[16,8,400]{2,1,0:T(8,128)}), f32[16,8,400]{2,1,0:T(8,128)S(1)}, u32[]{:S(2)}, u32[]{:S(2)}) async-start(f32[16,8,400]{2,1,0:T(8,128)} %broadcast_in_dim.10), calls=%async_computation.3 | async-start | bytes 524288 | tf_op jit(solution)/shard_map/all_to_all | solution.py:329
where the time goes:
time: 93.8 us; the launch traced here: 93 us
  waiting for transfers between devices  23.9 us (25%)
  starting transfers between devices  21.1 us (22%)
  local copies, waits for them, and re-layouts  18.2 us (19%)
  blocking collectives  16.1 us (17%)
  Pallas kernels  11.8 us (13%)
  other arithmetic  0.95 us (1%)
    all_to_all x1, blocking collectives, per_device(): lax.all_to_all(blocks, 'fibre', split_axis=0, concat_axis=0, tiled=True)  16.1 us
    all_to_all x1, waiting for transfers between devices, per_device(): lax.all_to_all(local_taps.reshape(count, 8, share // 8), 'fibre', split_a...  9.66 us
    all_to_all x1, starting transfers between devices, per_device(): got = lax.all_to_all(sent, 'fibre', split_axis=0, concat_axis=0, tiled=True)  9.63 us
    all_to_all x1, waiting for transfers between devices, per_device(): got = lax.all_to_all(sent, 'fibre', split_axis=0, concat_axis=0, tiled=True)  7.83 us
    all_to_all x1, waiting for transfers between devices, per_device(): lax.all_to_all(jnp.broadcast_to(part[None], (count, 8, share // 8)), 'fib...  6.42 us
    unnamed x28, local copies, waits for them, and re-layouts  5.96 us
    pallas_call x1, Pallas kernels, per_device(): call(filter_body, [shape((2, chans * outer, lanes), f32), shape((count, g...  5.47 us
    all_to_all x1, starting transfers between devices, per_device(): lax.all_to_all(local_taps.reshape(count, 8, share // 8), 'fibre', split_a...  3.54 us
  transfers between devices with their start and end apart: 5, of which 3 were waited for; matrix products, arithmetic and copies ran while one was open for 10% of the time, Pallas kernels for 2%

commit v1 on v0

v1 whole, which is shorter than its diff:
```python
import math

import jax
import jax.numpy as jnp
import numpy as np
from jax import lax
from jax.experimental import pallas as pl
from jax.experimental.pallas import tpu as pltpu
from jax.sharding import PartitionSpec as P

inv_root_two = 1.0 / math.sqrt(2.0)
inv_root_tau = 1.0 / math.sqrt(2.0 * math.pi)
lanes = 128
f32 = jnp.float32
bf16 = jnp.bfloat16
vmem_bytes = 50 * 1024 * 1024


def log2(size):
    bits = size.bit_length() - 1
    assert 1 << bits == size
    return bits


def dot(left, right):
    return jnp.dot(left, right, preferred_element_type=f32)


def one_hot(rows, cols, wanted):
    axis = 0 if wanted.shape[0] == 1 else 1
    index = lax.broadcasted_iota(jnp.int32, (rows, cols), axis)
    return jnp.where(index == wanted, 1.0, 0.0).astype(bf16)


def swap_rows(outer, inner):
    count = outer * inner
    row = lax.broadcasted_iota(jnp.int32, (count, 1), 0)
    source = (row & (inner - 1)) * outer + (row >> log2(inner))
    return one_hot(count, count, source)


def split(values):
    high = values.astype(bf16)
    return high, (values - high.astype(f32)).astype(bf16)


def dot_split(left, right):
    return dot(left[0], right[0]) + (dot(left[0], right[1]) + dot(left[1], right[0]))


def dft_tables(outer, th):
    waves = outer * lanes
    turn = 2.0 * math.pi
    a = np.arange(outer)
    b = np.arange(lanes)
    ang = turn * ((a[:, None] * a[None, :]) % outer) / outer
    eye = np.eye(th)
    o1 = np.concatenate([np.kron(np.cos(ang), eye), -np.kron(np.sin(ang), eye)], axis=0)
    ang = turn * ((b[:, None] * b[None, :]) % lanes) / lanes
    i2 = np.block([[np.cos(ang), -np.sin(ang)], [np.sin(ang), np.cos(ang)]])
    ang = np.repeat(turn * (a[:, None] * b[None, :]) / waves, th, axis=0)

    def halves(table):
        table = table.astype(np.float32)
        high = table.astype(bf16)
        return np.stack([high, (table - high.astype(np.float32)).astype(bf16)])

    return (
        halves(o1),
        halves(o1.T),
        halves(i2),
        halves(i2.T),
        np.cos(ang).astype(np.float32),
        np.sin(ang).astype(np.float32),
    )


MESH = pl.DeviceIdType.MESH


def section_kernel(dims, *refs):
    (cin, tw, ks, cout, th, chans, count, cuts) = dims
    (x_ref, cot_ref, w_ref, v_ref, re_ref, im_ref) = refs[:6]
    table_refs = refs[6:12]
    (dx_ref, fg_ref, tap_ref) = refs[12:15]
    (o1_ref, o1b_ref, i2_ref, i2b_ref, tc_ref, ts_ref) = held = refs[15:21]
    (lo_ref, hi_ref, pp_ref, ct_ref, sent_ref, gotx_ref, gotc_ref) = refs[21:28]
    (back_ref, grad_ref, gt_ref, gg_ref, xo_ref, part_ref, term_ref, whole_ref) = refs[28:36]
    (table_sem, halo_send, halo_recv, c_send, c_recv, x_send, x_recv) = refs[36:43]
    (g_send, g_recv, t_send, t_recv, w_send, w_recv) = refs[43:49]
    me = lax.axis_index("fibre")
    width = x_ref.shape[1]
    half = width // 2
    per = half // lanes
    outer = count * per
    rows = outer * th
    waves = outer * lanes
    group = chans * th

    def peer_of(k):
        return lax.rem(me + k, count)

    barrier = pltpu.get_barrier_semaphore()

    def greet(k, carry):
        pl.semaphore_signal(
            barrier, inc=1, device_id={"fibre": peer_of(k)}, device_id_type=MESH
        )
        return carry

    lax.fori_loop(1, count, greet, 0)
    loads = [
        pltpu.make_async_copy(src, dst, table_sem.at[i])
        for i, (src, dst) in enumerate(zip(table_refs, held))
    ]
    for load in loads:
        load.start()
    pl.semaphore_wait(barrier, count - 1)

    def remote(src, dst, ssem, rsem, peer):
        return pltpu.make_async_remote_copy(
            src_ref=src,
            dst_ref=dst,
            send_sem=ssem,
            recv_sem=rsem,
            device_id={"fibre": peer},
            device_id_type=MESH,
        )

    def exchange(src, dst, ssem, rsem):
        def copy(k):
            peer = peer_of(k)
            return remote(src.at[peer], dst.at[me], ssem.at[k], rsem.at[k], peer)

        def go(k, carry):
            copy(k).start()
            return carry

        def end(k, carry):
            copy(k).wait()
            return carry

        lax.fori_loop(1, count, go, 0)
        return lambda: lax.fori_loop(1, count, end, 0)

    to_right = remote(
        x_ref.at[:, width - lanes : width], lo_ref, halo_send.at[0], halo_recv.at[0], peer_of(1)
    )
    to_left = remote(
        x_ref.at[:, 0:lanes], hi_ref, halo_send.at[1], halo_recv.at[1], peer_of(count - 1)
    )
    to_right.start()
    to_left.start()
    end_cot = exchange(cot_ref, gotc_ref, c_send, c_recv)
    gotc_ref[me] = cot_ref[me]

    order = swap_rows(tw, cin)
    x2 = dot(order, x_ref[...]).astype(bf16)
    blank = jnp.zeros((2 * ks * cin, half), bf16)
    pp_ref[0 : 2 * ks * cin, :] = blank
    pp_ref[(tw + 2) * ks * cin : (tw + 4) * ks * cin, :] = blank
    to_right.wait()
    to_left.wait()
    lo2 = dot(order, lo_ref[...]).astype(bf16)
    hi2 = dot(order, hi_ref[...]).astype(bf16)
    for j in range(ks):
        m = 2 * lax.broadcasted_iota(jnp.int32, (1, half), 1) + (j - 2)
        pj = dot(x2, one_hot(width, half, m))
        if j < 2:
            pj += dot(lo2, one_hot(lanes, half, jnp.where((m < 0) & (me > 0), lanes + m, -1)))
        if j > 3:
            inside = (m >= width) & (me < count - 1)
            pj += dot(hi2, one_hot(lanes, half, jnp.where(inside, m - width, -1)))
        pj = pj.astype(bf16)
        for s in range(tw):
            at = ((s + 2) * ks + j) * cin
            pp_ref[at : at + cin, :] = pj[s * cin : (s + 1) * cin, :]
    step = 2 * ks * cin
    taps_rows = ks * ks * cin
    for t in range(th):
        patches = pp_ref[t * step : t * step + taps_rows, :]
        ct_ref[t * cout : (t + 1) * cout, :] = dot(w_ref[...], patches).astype(bf16)
    conv_out = dot(swap_rows(cout, th), ct_ref[...]).astype(bf16)
    sent_ref[...] = conv_out.reshape(count, group, half)
    end_conv = exchange(sent_ref, gotx_ref, x_send, x_recv)
    gotx_ref[me] = sent_ref[me]
    for load in loads:
        load.wait()
    end_cot()

    o1 = (o1_ref[0], o1_ref[1])
    o1b = (o1b_ref[0], o1b_ref[1])
    i2 = (i2_ref[0], i2_ref[1])
    i2b = (i2b_ref[0], i2b_ref[1])
    tcos = tc_ref[...]
    tsin = ts_ref[...]

    def gathered(ref):
        cols = []
        whole = [ref[d].astype(f32) for d in range(count)]
        for c in range(chans):
            tiles = []
            for d in range(count):
                at = c * th
                for h in range(per):
                    tiles.append(whole[d][at : at + th, h * lanes : (h + 1) * lanes])
            cols.append(jnp.concatenate(tiles, axis=0))
        return jnp.concatenate(cols, axis=1)

    def forward(first):
        wide = []
        for c in range(chans):
            fr = first[:rows, c * lanes : (c + 1) * lanes]
            fi = first[rows:, c * lanes : (c + 1) * lanes]
            wide.append(jnp.concatenate([fr * tcos + fi * tsin, fi * tcos - fr * tsin], axis=1))
        spec = dot_split(split(jnp.concatenate(wide, axis=0)), i2)
        return spec[:, :lanes], spec[:, lanes:]

    def backward(sr, si):
        back = dot_split(split(jnp.concatenate([sr, si], axis=1)), i2b)
        cols = []
        for c in range(chans):
            br = back[c * rows : (c + 1) * rows, :lanes]
            bi = back[c * rows : (c + 1) * rows, lanes:]
            cols.append(jnp.concatenate([br * tcos - bi * tsin, bi * tcos + br * tsin], axis=0))
        return dot_split(o1b, split(jnp.concatenate(cols, axis=1))) * (1.0 / waves)

    def spread(ref):
        flat = ref[...]
        return jnp.broadcast_to(flat[:, None, :], (flat.shape[0], th, lanes)).reshape(
            flat.shape[0] * th, lanes
        )

    resp_r = spread(re_ref)
    resp_i = spread(im_ref)
    end_conv()
    x = gathered(gotx_ref).astype(bf16)
    sr, si = forward(dot(o1[0], x) + dot(o1[1], x))
    v = backward(resp_r * sr - resp_i * si, resp_r * si + resp_i * sr)
    slope = 0.5 * (1.0 + lax.erf(v * inv_root_two)) + v * jnp.exp(-0.5 * v * v) * inv_root_tau
    g = gathered(gotc_ref) * slope
    gr, gi = forward(dot_split(o1, split(g)))
    scale = 1.0 / waves
    fg_ref[0] = jnp.sum((sr * gr + si * gi).reshape(chans * outer, th, lanes), axis=1) * scale
    fg_ref[1] = jnp.sum((sr * gi - si * gr).reshape(chans * outer, th, lanes), axis=1) * scale
    y = backward(resp_r * gr + resp_i * gi, resp_r * gi - resp_i * gr)
    lane = lax.broadcasted_iota(jnp.int32, (th, lanes), 1)
    zero = jnp.zeros((th, lanes), f32)
    for d in range(count):
        parts = []
        for c in range(chans):
            col = y[:, c * lanes : (c + 1) * lanes]
            low = col[(d * per - 1) * th : d * per * th] if d > 0 else zero
            high = col[(d + 1) * per * th : ((d + 1) * per + 1) * th] if d < count - 1 else zero
            rim = jnp.where(lane == lanes - 1, low, jnp.where(lane == 0, high, 0.0))
            tiles = [col[(d * per + h) * th : (d * per + h + 1) * th] for h in range(per)]
            parts.append(jnp.concatenate(tiles + [rim], axis=1))
        back_ref[d] = jnp.concatenate(parts, axis=0).astype(bf16)
    end_grad = exchange(back_ref, grad_ref, g_send, g_recv)
    grad_ref[me] = back_ref[me]
    end_grad()

    ext = half + lanes
    g_all = grad_ref[...].reshape(cout * th, ext)
    gt_ref[...] = dot(swap_rows(th, cout), g_all).astype(bf16)
    total = None
    for t in range(th):
        term = lax.dot_general(
            gt_ref[t * cout : (t + 1) * cout, :half],
            pp_ref[t * step : t * step + taps_rows, :],
            (((1,), (1,)), ((), ())),
            preferred_element_type=f32,
        )
        total = term if total is None else total + term
    part_width = part_ref.shape[2]
    total = jnp.concatenate(
        [total, jnp.zeros((cout, cuts * part_width - taps_rows), f32)], axis=1
    )
    for r in range(cout // 8):
        for p in range(cuts):
            part_ref[r * cuts + p] = total[
                r * 8 : (r + 1) * 8, p * part_width : (p + 1) * part_width
            ]
    end_terms = exchange(part_ref, term_ref, t_send, t_recv)
    term_ref[me] = part_ref[me]

    blank = jnp.zeros((3 * cout, half), bf16)
    gg_ref[0 : 3 * cout, :] = blank
    gg_ref[(th + 1) * 3 * cout : (th + 2) * 3 * cout, :] = blank
    p = lax.broadcasted_iota(jnp.int32, (1, half), 1)
    g2 = gt_ref[...]
    for sh in range(3):
        if sh == 1:
            moved = g2[:, :half]
        else:
            source = p + 1 if sh == 0 else jnp.where(p == 0, ext - 1, p - 1)
            moved = dot(g2, one_hot(ext, half, source)).astype(bf16)
        for t in range(th):
            at = ((t + 1) * 3 + sh) * cout
            gg_ref[at : at + cout, :] = moved[t * cout : (t + 1) * cout, :]

    end_terms()
    whole_ref[me] = jnp.sum(term_ref[...], axis=0) * (1.0 / math.sqrt(th * waves))

    def share(k):
        return remote(whole_ref.at[me], whole_ref.at[me], w_send.at[k], w_recv.at[k], peer_of(k))

    def share_start(k, carry):
        share(k).start()
        return carry

    def share_end(k, carry):
        share(k).wait()
        return carry

    lax.fori_loop(1, count, share_start, 0)

    for q in range(th):
        dx = lax.dot_general(
            v_ref[...],
            gg_ref[q * 3 * cout : (q + 3) * 3 * cout, :],
            (((0,), (0,)), ((), ())),
            preferred_element_type=f32,
        ).astype(bf16)
        for ps in range(2):
            for pm in range(2):
                at = (ps * 2 + pm) * cin
                row = (2 * q + ps) * cin
                xo_ref[row : row + cin, pm * half : (pm + 1) * half] = dx[at : at + cin, :]
    m = lax.broadcasted_iota(jnp.int32, (1, width), 1)
    weave = one_hot(width, width, (m & 1) * half + (m >> 1))
    woven = dot(xo_ref[...], weave).astype(bf16)
    dx_ref[...] = dot(swap_rows(cin, tw), woven).astype(bf16)
    lax.fori_loop(1, count, share_end, 0)
    tap_ref[...] = whole_ref[...]


def phase_weights(conv_taps):
    ks, _, cout, cin = conv_taps.shape
    none = jnp.zeros((cout, cin), conv_taps.dtype)
    cols = []
    for ps in range(2):
        for pm in range(2):
            rows = []
            for ti in range(3):
                i = (None, 3, 1)[ti] if ps else 4 - 2 * ti
                for sh in range(3):
                    j = 2 * sh + pm
                    rows.append(conv_taps[i, j] if i is not None and j < ks else none)
            cols.append(jnp.concatenate(rows, axis=0))
    return jnp.concatenate(cols, axis=1)


def per_device(signal, conv_taps, response, cotangent):
    ks, _, cout, cin = conv_taps.shape
    tw, width = signal.shape[1:]
    th, half = cotangent.shape[1:]
    count = lax.axis_size("fibre")
    chans = response.shape[1]
    waves = response.shape[2]
    outer = waves // lanes
    group = chans * th
    taps_rows = ks * ks * cin
    parts = count * 8 // cout
    assert parts * cout == count * 8
    part_width = -(-taps_rows // (parts * lanes)) * lanes
    shape = jax.ShapeDtypeStruct
    taps_flat = conv_taps.transpose(2, 0, 1, 3).reshape(cout, taps_rows)
    tables = dft_tables(outer, th)
    arranged = response.reshape(2, chans, lanes, outer).transpose(0, 1, 3, 2)
    arranged = arranged.reshape(2, chans * outer, lanes)
    dims = (cin, tw, ks, cout, th, chans, count, parts)

    def body(*refs):
        section_kernel(dims, *refs)

    vmem = pl.BlockSpec(memory_space=pltpu.VMEM)
    every = pltpu.SemaphoreType.DMA((count,))
    ext = half + lanes
    dx, fgrad, taps = pl.pallas_call(
        body,
        out_shape=[
            shape((cin * tw, width), bf16),
            shape((2, chans * outer, lanes), f32),
            shape((count, 8, part_width), f32),
        ],
        in_specs=[vmem] * 6 + [pl.BlockSpec(memory_space=pl.ANY)] * 6,
        out_specs=[vmem] * 3,
        scratch_shapes=[pltpu.VMEM(table.shape, table.dtype) for table in tables]
        + [
            pltpu.VMEM((cin * tw, lanes), bf16),
            pltpu.VMEM((cin * tw, lanes), bf16),
            pltpu.VMEM(((tw + 4) * ks * cin, half), bf16),
            pltpu.VMEM((cout * th, half), bf16),
            pltpu.VMEM((count, group, half), bf16),
            pltpu.VMEM((count, group, half), bf16),
            pltpu.VMEM((count, group, half), bf16),
            pltpu.VMEM((count, group, ext), bf16),
            pltpu.VMEM((count, group, ext), bf16),
            pltpu.VMEM((cout * th, ext), bf16),
            pltpu.VMEM(((th + 2) * 3 * cout, half), bf16),
            pltpu.VMEM((cin * tw, width), bf16),
            pltpu.VMEM((count, 8, part_width), f32),
            pltpu.VMEM((count, 8, part_width), f32),
            pltpu.VMEM((count, 8, part_width), f32),
            pltpu.SemaphoreType.DMA((6,)),
            pltpu.SemaphoreType.DMA((2,)),
            pltpu.SemaphoreType.DMA((2,)),
        ]
        + [every] * 10,
        compiler_params=pltpu.CompilerParams(
            vmem_limit_bytes=vmem_bytes, collective_id=0, has_side_effects=True
        ),
        cost_estimate=pl.CostEstimate(
            flops=6000000000, bytes_accessed=8000000, transcendentals=0
        ),
    )(
        signal.reshape(cin * tw, width),
        cotangent.reshape(count, group, half),
        taps_flat,
        phase_weights(conv_taps),
        arranged[0],
        arranged[1],
        *tables,
    )
    filter_grad = (
        fgrad.reshape(2, chans, outer, lanes).transpose(0, 1, 3, 2).reshape(2, chans, waves)
    )
    tap_grad = (
        taps.reshape(cout // 8, parts, 8, part_width)
        .transpose(0, 2, 1, 3)
        .reshape(cout, parts * part_width)[:, :taps_rows]
        .reshape(cout, ks, ks, cin)
        .transpose(1, 2, 0, 3)
    )
    return (dx.reshape(signal.shape), tap_grad, filter_grad)


def solution(mesh):
    in_specs = (P("parts", None, "fibre"), P(), P(None, "fibre", None), P("parts", None, "fibre"))
    out_specs = (P("parts", None, "fibre"), P("parts", None, None, None), P("parts", "fibre", None))
    return jax.shard_map(
        per_device, mesh=mesh, in_specs=in_specs, out_specs=out_specs, check_vma=False
    )
```

time: 93.8 us -> 65.1 us (0.69)
  Pallas kernels: 11.8 us -> 52.7 us
  waiting for transfers between devices: 23.9 us -> 0 us
  starting transfers between devices: 21.1 us -> 0 us
  blocking collectives: 16.1 us -> 0 us
  local copies, waits for them, and re-layouts: 18.2 us -> 10.8 us
    pallas_call x4 -> x1, Pallas kernels: 11.8 us -> 52.7 us  [per_device(): pl.pallas_call(body, out_shape=[shape((cin * tw, width), bf16), shape((2,...]
    all_to_all x3 -> x0, waiting for transfers between devices: 23.9 us -> none  [the longest x1 9.66 us: per_device(): lax.all_to_all(local_taps.reshape(count, 8, share // 8), 'fibre', split_a...]
    all_to_all x3 -> x0, starting transfers between devices: 16.7 us -> none  [the longest x1 9.63 us: per_device(): got = lax.all_to_all(sent, 'fibre', split_axis=0, concat_axis=0, tiled=True)]
    all_to_all x1 -> x0, blocking collectives: 16.1 us -> none  [per_device(): lax.all_to_all(blocks, 'fibre', split_axis=0, concat_axis=0, tiled=True)]
    ppermute x2 -> x0, starting transfers between devices: 4.44 us -> none  [the longest x1 3.15 us: per_device(): low = lax.ppermute(signal[:, :, width - 2:], 'fibre', up)]
    unnamed x28 -> x22, local copies, waits for them, and re-layouts: 5.96 us -> 2.47 us
    reshape x1, local copies, waits for them, and re-layouts: 2 us -> 0.18 us  [per_device(): arranged = response.reshape(2, chans, lanes, outer).transpose(0, 1, 3, 2)]
    reshape x3 -> x2, local copies, waits for them, and re-layouts: 2.27 us -> 1.26 us  [the longest x1 1.06 us: per_device(): taps_flat = conv_taps.transpose(2, 0, 1, 3).reshape(cout, taps_rows)]
  transfers between devices with their start and end apart: 5 -> 0, of which waited for: 3 -> 0; matrix products, arithmetic and copies ran while one was open for 10% -> 0% of each run, Pallas kernels for 2% -> 0%
where the time goes in v1:
time: 65.1 us; the launch traced here: 64.5 us
  Pallas kernels  52.7 us (81%)
  local copies, waits for them, and re-layouts  10.8 us (17%)
  between operations  0.83 us (1%)
    pallas_call x1, Pallas kernels, per_device(): pl.pallas_call(body, out_shape=[shape((cin * tw, width), bf16), shape((2,...  52.7 us
    unnamed x22, local copies, waits for them, and re-layouts  2.47 us
    slice x2, local copies, waits for them, and re-layouts, per_device(): arranged[1]  1.93 us

profile of v1, /device:TPU:0, one launch (start us, length us, event | category | flops | bytes accessed | tf_op | source)
XLA Modules:
  0.0 64.5 jit_solution(12241943863705278773)
XLA Ops:
  0.6 0.0 copy-start.8
  0.6 0.8 %slice_bitcast_fusion.21 = (bf16[64,32]{0,1:T(8,128)(2,1)S(1)}, bf16[64,32]{0,1:T(8,128)(2,1)S(1)}, bf16[64,32]{0,1:T(8,128)(2,1)S(1)}, bf16[64,32]{0,1:T(8,128)...) fusion(bf16[5,5,64,32]{2,3,1,0:T(8,128)(2,1)} %param.11), kind=kLoop, calls=%fused_computation.23 | loop fusion | bytes 49152 | tf_op jit(solution)/shard_map/squeeze | solution.py:349
  1.5 1.1 %copy.109.refs_2_ = bf16[64,800]{1,0:T(8,128)(2,1)S(1)} copy(bf16[64,800]{0,1:T(8,128)(2,1)} %bitcast.84) | data formatting | bytes 204800 | tf_op jit(solution)/shard_map/reshape | solution.py:368
  2.6 0.1 concatenate.15
  2.7 0.1 concatenate.18
  2.8 0.1 concatenate.17
  2.9 0.1 concatenate.16
  3.0 0.1 copy.104
  3.1 0.1 copy.105
  3.3 0.1 copy.106
  3.4 0.1 copy.103
  3.6 0.0 copy-start.9
  3.6 0.0 copy-start.6
  3.6 0.2 pad_maximum_fusion.refs_3_
  3.8 0.7 %copy-done.9 = f32[2,4,4096]{2,1,0:T(4,128)S(1)} copy-done((f32[2,4,4096]{2,1,0:T(4,128)S(1)}, f32[2,4,4096]{2,1,0:T(4,128)}, u32[]{:S(2)}) %copy-start.9) | copy-done | bytes 131096
  4.5 0.2 reshape.44
  4.7 0.0 copy-start.1
  4.7 0.0 copy-start.2
  4.7 0.0 copy-start.4
  4.7 0.8 %fusion = (f32[1,4,32,128]{2,3,1,0:T(8,128)}, f32[1,4,32,128]{2,3,1,0:T(8,128)}) fusion(f32[2,4,32,128]{2,3,1,0:T(8,128)S(1)} %bitcast.81), kind=kLoop, calls=%fused_computation.27 | loop fusion | bytes 262144 | tf_op jit(solution)/shard_map/slice | solution.py:423
  5.6 1.1 %copy.108 = f32[1,4,32,128]{3,2,1,0:T(8,128)S(1)} copy(f32[1,4,32,128]{2,3,1,0:T(8,128)} %get-tuple-element.9) | data formatting | bytes 131072 | tf_op jit(solution)/shard_map/slice | solution.py:423
  6.7 1.1 %copy.107 = f32[1,4,32,128]{3,2,1,0:T(8,128)S(1)} copy(f32[1,4,32,128]{2,3,1,0:T(8,128)} %get-tuple-element.10) | data formatting | bytes 131072 | tf_op jit(solution)/shard_map/slice | solution.py:422
  7.7 0.0 copy-done.6
  7.7 0.0 copy-done.3
  7.8 0.0 copy-start.7
  7.8 0.9 %copy-done.7 = f32[256,128]{1,0:T(8,128)S(1)} copy-done((f32[256,128]{1,0:T(8,128)S(1)}, f32[256,128]{1,0:T(8,128)}, u32[]{:S(2)}) %copy-start.7) | copy-done | bytes 131096
  8.7 52.7 %shard_map.121 = (bf16[512,512]{1,0:T(8,128)(2,1)S(1)}, f32[2,128,128]{2,1,0:T(8,128)S(1)}, f32[16,8,512]{2,1,0:T(8,128)S(1)}) custom-call(bf16[512,512]{1,0:T(8,128)(2,1)S(1)} %bitcast.78, bf16[16,32,256]{2,1,0:T(8,128)(2,1)S(1)} %bitcast.79, bf16[64,800]{1,0:T(8,128)(2,1)S(1)} %copy.109.refs_2_, bf16[576,128]{1,0:T(8,128)(2,1)S(1)} %pad_maximum_fusion.refs_3_, ...), custom_call_target="tpu_custom_call" | custom-call | flops 6000000000 | bytes 8000000 | tf_op jit(solution)/shard_map/pallas_call | solution.py:380
  61.4 0.2 copy.115
  61.7 0.9 %copy.111 = f32[64,800]{0,1:T(8,128)} copy(f32[64,800]{1,0:T(8,128)S(1)} %slice.116) | data formatting | bytes 409600 | tf_op jit(solution)/shard_map/slice | solution.py:430
  62.6 0.2 copy.112
  62.8 0.9 %reshape.50 = f32[2,4,4096]{2,1,0:T(4,128)} reshape(f32[2,4,128,32]{3,2,1,0:T(8,128)S(1)} %bitcast.80) | data formatting | bytes 262144 | tf_op jit(solution)/shard_map/reshape | solution.py:427
  63.8 0.8 %copy.117 = bf16[32,16,512]{2,1,0:T(8,128)(2,1)} copy(bf16[32,16,512]{2,1,0:T(8,128)(2,1)S(1)} %bitcast.73) | data formatting | bytes 1048576
  (14 shorter events, 0.1 us)
Async XLA Ops:
  0.6 1.9 %copy-start.8 = (bf16[5,5,64,32]{2,3,1,0:T(8,128)(2,1)S(1)}, bf16[5,5,64,32]{2,3,1,0:T(8,128)(2,1)}, u32[]{:S(2)}) copy-start(bf16[5,5,64,32]{2,3,1,0:T(8,128)(2,1)} %param.11) | copy-start | bytes 307204
  3.6 0.9 %copy-start.9 = (f32[2,4,4096]{2,1,0:T(4,128)S(1)}, f32[2,4,4096]{2,1,0:T(4,128)}, u32[]{:S(2)}) copy-start(f32[2,4,4096]{2,1,0:T(4,128)} %param.12) | copy-start | bytes 393220
  3.6 4.1 %copy-start.6 = (f32[256,128]{1,0:T(8,128)S(1)}, f32[256,128]{1,0:T(8,128)}, u32[]{:S(2)}) copy-start(f32[256,128]{1,0:T(8,128)} %constant.20.clone.refs_11_) | copy-start | bytes 393220
  4.5 3.2 %copy-start.3 = (bf16[2,512,256]{2,1,0:T(8,128)(2,1)S(1)}, bf16[2,512,256]{2,1,0:T(8,128)(2,1)}, u32[]{:S(2)}) copy-start(bf16[2,512,256]{2,1,0:T(8,128)(2,1)} %constant.6.clone.refs_6_) | copy-start | bytes 1572868
  4.5 3.2 %copy-start.5 = (bf16[2,256,256]{2,1,0:T(8,128)(2,1)S(1)}, bf16[2,256,256]{2,1,0:T(8,128)(2,1)}, u32[]{:S(2)}) copy-start(bf16[2,256,256]{2,1,0:T(8,128)(2,1)} %constant.17.clone.refs_8_) | copy-start | bytes 786436
  4.7 3.1 %copy-start.1 = (bf16[64,8,256]{2,1,0:T(8,128)(2,1)S(1)}, bf16[64,8,256]{2,1,0:T(8,128)(2,1)}, u32[]{:S(2)}) copy-start(bf16[64,8,256]{2,1,0:T(8,128)(2,1)} %param.13) | copy-start | bytes 786436
  4.7 3.1 %copy-start.2 = (bf16[2,256,512]{2,1,0:T(8,128)(2,1)S(1)}, bf16[2,256,512]{2,1,0:T(8,128)(2,1)}, u32[]{:S(2)}) copy-start(bf16[2,256,512]{2,1,0:T(8,128)(2,1)} %constant.16.clone.refs_7_) | copy-start | bytes 1572868
  4.7 3.1 %copy-start.4 = (bf16[2,256,256]{2,1,0:T(8,128)(2,1)S(1)}, bf16[2,256,256]{2,1,0:T(8,128)(2,1)}, u32[]{:S(2)}) copy-start(bf16[2,256,256]{2,1,0:T(8,128)(2,1)} %constant.18.clone.refs_9_) | copy-start | bytes 786436
  5.6 2.2 %copy-start = (bf16[32,16,512]{2,1,0:T(8,128)(2,1)S(1)}, bf16[32,16,512]{2,1,0:T(8,128)(2,1)}, u32[]{:S(2)}) copy-start(bf16[32,16,512]{2,1,0:T(8,128)(2,1)} %param.10) | copy-start | bytes 1572868
  7.8 0.9 %copy-start.7 = (f32[256,128]{1,0:T(8,128)S(1)}, f32[256,128]{1,0:T(8,128)}, u32[]{:S(2)}) copy-start(f32[256,128]{1,0:T(8,128)} %constant.19.clone.refs_10_) | copy-start | bytes 393220

commit v2 on v1

--- a/solution.py
+++ b/solution.py
@@ -80,14 +80,15 @@
 
 def section_kernel(dims, *refs):
     (cin, tw, ks, cout, th, chans, count, cuts) = dims
-    (x_ref, cot_ref, w_ref, v_ref, re_ref, im_ref) = refs[:6]
-    table_refs = refs[6:12]
-    (dx_ref, fg_ref, tap_ref) = refs[12:15]
-    (o1_ref, o1b_ref, i2_ref, i2b_ref, tc_ref, ts_ref) = held = refs[15:21]
-    (lo_ref, hi_ref, pp_ref, ct_ref, sent_ref, gotx_ref, gotc_ref) = refs[21:28]
-    (back_ref, grad_ref, gt_ref, gg_ref, xo_ref, part_ref, term_ref, whole_ref) = refs[28:36]
-    (table_sem, halo_send, halo_recv, c_send, c_recv, x_send, x_recv) = refs[36:43]
-    (g_send, g_recv, t_send, t_recv, w_send, w_recv) = refs[43:49]
+    (x_ref, cot_ref, w_ref, resp_ref) = refs[:4]
+    table_refs = refs[4:10]
+    (dx_ref, fg_ref, tap_ref) = refs[10:13]
+    (o1_ref, o1b_ref, i2_ref, i2b_ref, tc_ref, ts_ref) = held = refs[13:19]
+    (lo_ref, hi_ref, pp_ref, ct_ref, sent_ref, gotx_ref, gotc_ref) = refs[19:26]
+    (back_ref, grad_ref, gt_ref, gg_ref, xo_ref, part_ref, term_ref, whole_ref) = refs[26:34]
+    (glo_ref, ghi_ref, v_ref) = refs[34:37]
+    (table_sem, halo_send, halo_recv, c_send, c_recv, x_send, x_recv) = refs[37:44]
+    (g_send, g_recv, t_send, t_recv, w_send, w_recv) = refs[44:50]
     me = lax.axis_index("fibre")
     width = x_ref.shape[1]
     half = width // 2
@@ -127,7 +128,7 @@
             device_id_type=MESH,
         )
 
-    def exchange(src, dst, ssem, rsem):
+    def exchange(src, dst, ssem, rsem, last=count):
         def copy(k):
             peer = peer_of(k)
             return remote(src.at[peer], dst.at[me], ssem.at[k], rsem.at[k], peer)
@@ -140,8 +141,10 @@
             copy(k).wait()
             return carry
 
-        lax.fori_loop(1, count, go, 0)
-        return lambda: lax.fori_loop(1, count, end, 0)
+        lax.fori_loop(1, last, go, 0)
+        rest = lambda: lax.fori_loop(last, count, go, 0)
+        finish = lambda: lax.fori_loop(1, count, end, 0)
+        return (rest, finish) if last < count else finish
 
     to_right = remote(
         x_ref.at[:, width - lanes : width], lo_ref, halo_send.at[0], halo_recv.at[0], peer_of(1)
@@ -151,7 +154,7 @@
     )
     to_right.start()
     to_left.start()
-    end_cot = exchange(cot_ref, gotc_ref, c_send, c_recv)
+    more_cot, end_cot = exchange(cot_ref, gotc_ref, c_send, c_recv, count // 2)
     gotc_ref[me] = cot_ref[me]
 
     order = swap_rows(tw, cin)
@@ -179,14 +182,16 @@
     taps_rows = ks * ks * cin
     for t in range(th):
         patches = pp_ref[t * step : t * step + taps_rows, :]
-        ct_ref[t * cout : (t + 1) * cout, :] = dot(w_ref[...], patches).astype(bf16)
+        ct_ref[t * cout : (t + 1) * cout, :] = lax.dot_general(
+            w_ref[...], patches, (((0,), (0,)), ((), ())), preferred_element_type=f32
+        ).astype(bf16)
     conv_out = dot(swap_rows(cout, th), ct_ref[...]).astype(bf16)
     sent_ref[...] = conv_out.reshape(count, group, half)
     end_conv = exchange(sent_ref, gotx_ref, x_send, x_recv)
+    more_cot()
     gotx_ref[me] = sent_ref[me]
     for load in loads:
         load.wait()
-    end_cot()
 
     o1 = (o1_ref[0], o1_ref[1])
     o1b = (o1b_ref[0], o1b_ref[1])
@@ -225,48 +230,67 @@
             cols.append(jnp.concatenate([br * tcos - bi * tsin, bi * tcos + br * tsin], axis=0))
         return dot_split(o1b, split(jnp.concatenate(cols, axis=1))) * (1.0 / waves)
 
-    def spread(ref):
-        flat = ref[...]
+    def spread(at):
+        flat = jnp.concatenate([resp_ref[at, c].T for c in range(chans)], axis=0)
         return jnp.broadcast_to(flat[:, None, :], (flat.shape[0], th, lanes)).reshape(
             flat.shape[0] * th, lanes
         )
 
-    resp_r = spread(re_ref)
-    resp_i = spread(im_ref)
+    resp_r = spread(0)
+    resp_i = spread(1)
     end_conv()
     x = gathered(gotx_ref).astype(bf16)
     sr, si = forward(dot(o1[0], x) + dot(o1[1], x))
     v = backward(resp_r * sr - resp_i * si, resp_r * si + resp_i * sr)
     slope = 0.5 * (1.0 + lax.erf(v * inv_root_two)) + v * jnp.exp(-0.5 * v * v) * inv_root_tau
+    end_cot()
     g = gathered(gotc_ref) * slope
     gr, gi = forward(dot_split(o1, split(g)))
     scale = 1.0 / waves
-    fg_ref[0] = jnp.sum((sr * gr + si * gi).reshape(chans * outer, th, lanes), axis=1) * scale
-    fg_ref[1] = jnp.sum((sr * gi - si * gr).reshape(chans * outer, th, lanes), axis=1) * scale
     y = backward(resp_r * gr + resp_i * gi, resp_r * gi - resp_i * gr)
-    lane = lax.broadcasted_iota(jnp.int32, (th, lanes), 1)
-    zero = jnp.zeros((th, lanes), f32)
     for d in range(count):
-        parts = []
+        blocks = []
         for c in range(chans):
             col = y[:, c * lanes : (c + 1) * lanes]
-            low = col[(d * per - 1) * th : d * per * th] if d > 0 else zero
-            high = col[(d + 1) * per * th : ((d + 1) * per + 1) * th] if d < count - 1 else zero
-            rim = jnp.where(lane == lanes - 1, low, jnp.where(lane == 0, high, 0.0))
             tiles = [col[(d * per + h) * th : (d * per + h + 1) * th] for h in range(per)]
-            parts.append(jnp.concatenate(tiles + [rim], axis=1))
-        back_ref[d] = jnp.concatenate(parts, axis=0).astype(bf16)
+            blocks.append(jnp.concatenate(tiles, axis=1))
+        back_ref[d] = jnp.concatenate(blocks, axis=0).astype(bf16)
     end_grad = exchange(back_ref, grad_ref, g_send, g_recv)
     grad_ref[me] = back_ref[me]
+    scale = 1.0 / waves
+    crosses = (sr * gr + si * gi, sr * gi - si * gr)
+    for at, cross in enumerate(crosses):
+        summed = jnp.sum(cross.reshape(chans * outer, th, lanes), axis=1) * scale
+        for c in range(chans):
+            fg_ref[at, c] = summed[c * outer : (c + 1) * outer].T
+    v_ref[...] = jnp.zeros(v_ref.shape, f32)
+    for ps in range(2):
+        for pm in range(2):
+            for ti in range(3):
+                i = (None, 3, 1)[ti] if ps else 4 - 2 * ti
+                for sh in range(3):
+                    j = 2 * sh + pm
+                    if i is not None and j < ks:
+                        row = (ps * 2 + pm) * cin
+                        col = (ti * 3 + sh) * cout
+                        at = (i * ks + j) * cin
+                        v_ref[row : row + cin, col : col + cout] = w_ref[at : at + cin, :].astype(f32)
     end_grad()
 
-    ext = half + lanes
-    g_all = grad_ref[...].reshape(cout * th, ext)
+    g_all = grad_ref[...].reshape(cout * th, half)
     gt_ref[...] = dot(swap_rows(th, cout), g_all).astype(bf16)
+    g_right = remote(
+        gt_ref.at[:, half - lanes : half], glo_ref, halo_send.at[2], halo_recv.at[2], peer_of(1)
+    )
+    g_left = remote(
+        gt_ref.at[:, 0:lanes], ghi_ref, halo_send.at[3], halo_recv.at[3], peer_of(count - 1)
+    )
+    g_right.start()
+    g_left.start()
     total = None
     for t in range(th):
         term = lax.dot_general(
-            gt_ref[t * cout : (t + 1) * cout, :half],
+            gt_ref[t * cout : (t + 1) * cout, :],
             pp_ref[t * step : t * step + taps_rows, :],
             (((1,), (1,)), ((), ())),
             preferred_element_type=f32,
@@ -276,11 +300,11 @@
     total = jnp.concatenate(
         [total, jnp.zeros((cout, cuts * part_width - taps_rows), f32)], axis=1
     )
-    for r in range(cout // 8):
+    for r in range(cout // 16):
         for p in range(cuts):
             part_ref[r * cuts + p] = total[
-                r * 8 : (r + 1) * 8, p * part_width : (p + 1) * part_width
-            ]
+                r * 16 : (r + 1) * 16, p * part_width : (p + 1) * part_width
+            ].astype(bf16)
     end_terms = exchange(part_ref, term_ref, t_send, t_recv)
     term_ref[me] = part_ref[me]
 
@@ -289,18 +313,27 @@
     gg_ref[(th + 1) * 3 * cout : (th + 2) * 3 * cout, :] = blank
     p = lax.broadcasted_iota(jnp.int32, (1, half), 1)
     g2 = gt_ref[...]
+    g_right.wait()
+    g_left.wait()
     for sh in range(3):
-        if sh == 1:
-            moved = g2[:, :half]
+        if sh == 0:
+            rim = jnp.where((p == half - 1) & (me < count - 1), 0, -1)
+            moved = dot(g2, one_hot(half, half, p + 1))
+            moved = (moved + dot(ghi_ref[...], one_hot(lanes, half, rim))).astype(bf16)
+        elif sh == 1:
+            moved = g2
         else:
-            source = p + 1 if sh == 0 else jnp.where(p == 0, ext - 1, p - 1)
-            moved = dot(g2, one_hot(ext, half, source)).astype(bf16)
+            rim = jnp.where((p == 0) & (me > 0), lanes - 1, -1)
+            moved = dot(g2, one_hot(half, half, p - 1))
+            moved = (moved + dot(glo_ref[...], one_hot(lanes, half, rim))).astype(bf16)
         for t in range(th):
             at = ((t + 1) * 3 + sh) * cout
             gg_ref[at : at + cout, :] = moved[t * cout : (t + 1) * cout, :]
 
     end_terms()
-    whole_ref[me] = jnp.sum(term_ref[...], axis=0) * (1.0 / math.sqrt(th * waves))
+    whole_ref[me] = (
+        jnp.sum(term_ref[...].astype(f32), axis=0) * (1.0 / math.sqrt(th * waves))
+    ).astype(bf16)
 
     def share(k):
         return remote(whole_ref.at[me], whole_ref.at[me], w_send.at[k], w_recv.at[k], peer_of(k))
@@ -315,13 +348,9 @@
 
     lax.fori_loop(1, count, share_start, 0)
 
+    weights = v_ref[...].astype(bf16)
     for q in range(th):
-        dx = lax.dot_general(
-            v_ref[...],
-            gg_ref[q * 3 * cout : (q + 3) * 3 * cout, :],
-            (((0,), (0,)), ((), ())),
-            preferred_element_type=f32,
-        ).astype(bf16)
+        dx = dot(weights, gg_ref[q * 3 * cout : (q + 3) * 3 * cout, :]).astype(bf16)
         for ps in range(2):
             for pm in range(2):
                 at = (ps * 2 + pm) * cin
@@ -332,23 +361,7 @@
     woven = dot(xo_ref[...], weave).astype(bf16)
     dx_ref[...] = dot(swap_rows(cin, tw), woven).astype(bf16)
     lax.fori_loop(1, count, share_end, 0)
-    tap_ref[...] = whole_ref[...]
-
-
-def phase_weights(conv_taps):
-    ks, _, cout, cin = conv_taps.shape
-    none = jnp.zeros((cout, cin), conv_taps.dtype)
-    cols = []
-    for ps in range(2):
-        for pm in range(2):
-            rows = []
-            for ti in range(3):
-                i = (None, 3, 1)[ti] if ps else 4 - 2 * ti
-                for sh in range(3):
-                    j = 2 * sh + pm
-                    rows.append(conv_taps[i, j] if i is not None and j < ks else none)
-            cols.append(jnp.concatenate(rows, axis=0))
-    return jnp.concatenate(cols, axis=1)
+    tap_ref[...] = whole_ref[...].astype(f32)
 
 
 def per_device(signal, conv_taps, response, cotangent):
@@ -361,14 +374,12 @@
     outer = waves // lanes
     group = chans * th
     taps_rows = ks * ks * cin
-    parts = count * 8 // cout
-    assert parts * cout == count * 8
+    parts = count * 16 // cout
+    assert parts * cout == count * 16
     part_width = -(-taps_rows // (parts * lanes)) * lanes
     shape = jax.ShapeDtypeStruct
-    taps_flat = conv_taps.transpose(2, 0, 1, 3).reshape(cout, taps_rows)
+    taps_flat = conv_taps.transpose(0, 1, 3, 2).reshape(taps_rows, cout)
     tables = dft_tables(outer, th)
-    arranged = response.reshape(2, chans, lanes, outer).transpose(0, 1, 3, 2)
-    arranged = arranged.reshape(2, chans * outer, lanes)
     dims = (cin, tw, ks, cout, th, chans, count, parts)
 
     def body(*refs):
@@ -376,15 +387,14 @@
 
     vmem = pl.BlockSpec(memory_space=pltpu.VMEM)
     every = pltpu.SemaphoreType.DMA((count,))
-    ext = half + lanes
     dx, fgrad, taps = pl.pallas_call(
         body,
         out_shape=[
             shape((cin * tw, width), bf16),
-            shape((2, chans * outer, lanes), f32),
-            shape((count, 8, part_width), f32),
+            shape((2, chans, lanes, outer), f32),
+            shape((count, 16, part_width), f32),
         ],
-        in_specs=[vmem] * 6 + [pl.BlockSpec(memory_space=pl.ANY)] * 6,
+        in_specs=[vmem] * 4 + [pl.BlockSpec(memory_space=pl.ANY)] * 6,
         out_specs=[vmem] * 3,
         scratch_shapes=[pltpu.VMEM(table.shape, table.dtype) for table in tables]
         + [
@@ -395,17 +405,20 @@
             pltpu.VMEM((count, group, half), bf16),
             pltpu.VMEM((count, group, half), bf16),
             pltpu.VMEM((count, group, half), bf16),
-            pltpu.VMEM((count, group, ext), bf16),
-            pltpu.VMEM((count, group, ext), bf16),
-            pltpu.VMEM((cout * th, ext), bf16),
+            pltpu.VMEM((count, group, half), bf16),
+            pltpu.VMEM((count, group, half), bf16),
+            pltpu.VMEM((cout * th, half), bf16),
             pltpu.VMEM(((th + 2) * 3 * cout, half), bf16),
             pltpu.VMEM((cin * tw, width), bf16),
-            pltpu.VMEM((count, 8, part_width), f32),
-            pltpu.VMEM((count, 8, part_width), f32),
-            pltpu.VMEM((count, 8, part_width), f32),
+            pltpu.VMEM((count, 16, part_width), bf16),
+            pltpu.VMEM((count, 16, part_width), bf16),
+            pltpu.VMEM((count, 16, part_width), bf16),
+            pltpu.VMEM((cout * th, lanes), bf16),
+            pltpu.VMEM((cout * th, lanes), bf16),
+            pltpu.VMEM((4 * cin, 9 * cout), f32),
             pltpu.SemaphoreType.DMA((6,)),
-            pltpu.SemaphoreType.DMA((2,)),
-            pltpu.SemaphoreType.DMA((2,)),
+            pltpu.SemaphoreType.DMA((4,)),
+            pltpu.SemaphoreType.DMA((4,)),
         ]
         + [every] * 10,
         compiler_params=pltpu.CompilerParams(
@@ -418,16 +431,12 @@
         signal.reshape(cin * tw, width),
         cotangent.reshape(count, group, half),
         taps_flat,
-        phase_weights(conv_taps),
-        arranged[0],
-        arranged[1],
+        response.reshape(2, chans, lanes, outer),
         *tables,
     )
-    filter_grad = (
-        fgrad.reshape(2, chans, outer, lanes).transpose(0, 1, 3, 2).reshape(2, chans, waves)
-    )
+    filter_grad = fgrad.reshape(2, chans, waves)
     tap_grad = (
-        taps.reshape(cout // 8, parts, 8, part_width)
+        taps.reshape(cout // 16, parts, 16, part_width)
         .transpose(0, 2, 1, 3)
         .reshape(cout, parts * part_width)[:, :taps_rows]
         .reshape(cout, ks, ks, cin)

time: 65.1 us -> 60 us (0.922)
  Pallas kernels: 52.7 us -> 50.3 us
  local copies, waits for them, and re-layouts: 10.8 us -> 8.72 us
    unnamed x22 -> x16, local copies, waits for them, and re-layouts: 2.47 us -> 5.53 us
    slice x5 -> x2, local copies, waits for them, and re-layouts: 3.94 us -> 0.95 us  [per_device(): taps.reshape(cout // 16, parts, 16, part_width).transpose(0, 2, 1, 3)]
    pallas_call x1, Pallas kernels: 52.7 us -> 50.3 us  [per_device(): pl.pallas_call(body, out_shape=[shape((cin * tw, width), bf16), shape((2,...]
    concatenate x8 -> x0, local copies, waits for them, and re-layouts: 0.99 us -> none  [phase_weights(): cols.append(jnp.concatenate(rows, axis=0))]
    squeeze x2 -> x0, local copies, waits for them, and re-layouts: 0.84 us -> none  [phase_weights(): rows.append(conv_taps[i, j] if i is not None and j < ks else none)]
    reshape x5 -> x3, local copies, waits for them, and re-layouts: 2.56 us -> 2.24 us  [the longest x1 1.14 us: per_device(): response.reshape(2, chans, lanes, outer)]
where the time goes in v2:
time: 60 us; the launch traced here: 59.7 us
  Pallas kernels  50.3 us (84%)
  local copies, waits for them, and re-layouts  8.72 us (15%)
  between operations  0.71 us (1%)
    pallas_call x1, Pallas kernels, per_device(): pl.pallas_call(body, out_shape=[shape((cin * tw, width), bf16), shape((2,...  50.3 us
    unnamed x16, local copies, waits for them, and re-layouts  5.53 us

profile of v2, /device:TPU:0, one launch (start us, length us, event | category | flops | bytes accessed | tf_op | source)
XLA Modules:
  0.0 59.7 jit_solution(6681884357909342784)
XLA Ops:
  0.6 0.0 copy-start
  0.6 0.0 copy-start.5
  0.7 1.1 %reshape.36.refs_3_ = f32[2,4,128,32]{3,2,1,0:T(8,128)S(1)} reshape(f32[2,4,4096]{2,1,0:T(4,128)} %param.12) | data formatting | bytes 262144 | tf_op jit(solution)/shard_map/reshape | solution.py:434
  1.8 0.0 copy-done
  1.8 0.0 copy-done.5
  1.8 0.0 copy-start.1
  1.8 0.9 %copy-done.1 = bf16[64,8,256]{2,1,0:T(8,128)(2,1)S(1)} copy-done((bf16[64,8,256]{2,1,0:T(8,128)(2,1)S(1)}, bf16[64,8,256]{2,1,0:T(8,128)(2,1)}, u32[]{:S(2)}) %copy-start.1) | copy-done | bytes 262168
  2.8 0.0 copy-start.2
  2.8 0.9 %copy-done.2 = bf16[5,5,64,32]{2,3,1,0:T(8,128)(2,1)S(1)} copy-done((bf16[5,5,64,32]{2,3,1,0:T(8,128)(2,1)S(1)}, bf16[5,5,64,32]{2,3,1,0:T(8,128)(2,1)}, u32[]{:S(2)}) %copy-start.2) | copy-done | bytes 102424
  3.7 0.0 copy-start.3
  3.7 0.9 %copy-done.3 = bf16[2,256,256]{2,1,0:T(8,128)(2,1)S(1)} copy-done((bf16[2,256,256]{2,1,0:T(8,128)(2,1)S(1)}, bf16[2,256,256]{2,1,0:T(8,128)(2,1)}, u32[]{:S(2)}) %copy-start.3) | copy-done | bytes 262168
  4.7 0.0 copy-start.4
  4.7 0.9 %copy-done.4 = bf16[2,256,256]{2,1,0:T(8,128)(2,1)S(1)} copy-done((bf16[2,256,256]{2,1,0:T(8,128)(2,1)S(1)}, bf16[2,256,256]{2,1,0:T(8,128)(2,1)}, u32[]{:S(2)}) %copy-start.4) | copy-done | bytes 262168
  5.6 0.0 copy-start.6
  5.6 0.9 %copy-done.6 = f32[256,128]{1,0:T(8,128)S(1)} copy-done((f32[256,128]{1,0:T(8,128)S(1)}, f32[256,128]{1,0:T(8,128)}, u32[]{:S(2)}) %copy-start.6) | copy-done | bytes 131096
  6.5 50.3 %shard_map.121 = (bf16[512,512]{1,0:T(8,128)(2,1)S(1)}, f32[2,4,128,32]{3,2,1,0:T(8,128)S(1)}, f32[16,16,256]{2,1,0:T(8,128)S(1)}) custom-call(bf16[512,512]{1,0:T(8,128)(2,1)S(1)} %bitcast.18, bf16[16,32,256]{2,1,0:T(8,128)(2,1)S(1)} %bitcast.19, bf16[800,64]{1,0:T(8,128)(2,1)S(1)} %bitcast.20, f32[2,4,128,32]{3,2,1,0:T(8,128)S(1)} %reshape.36.refs_3_, ...), custom_call_target="tpu_custom_call" | custom-call | flops 6000000000 | bytes 8000000 | tf_op jit(solution)/shard_map/pallas_call | solution.py:390
  56.8 0.2 copy.15
  57.1 0.9 %reshape.41 = f32[2,4,4096]{2,1,0:T(4,128)} reshape(f32[2,4,128,32]{3,2,1,0:T(8,128)S(1)} %get-tuple-element.8) | data formatting | bytes 262144 | tf_op jit(solution)/shard_map/reshape | solution.py:437
  58.0 0.9 %copy.16 = f32[64,800]{0,1:T(8,128)} copy(f32[64,800]{1,0:T(8,128)S(1)} %slice.4) | data formatting | bytes 409600 | tf_op jit(solution)/shard_map/slice | solution.py:439
  58.9 0.8 %copy.19 = bf16[32,16,512]{2,1,0:T(8,128)(2,1)} copy(bf16[32,16,512]{2,1,0:T(8,128)(2,1)S(1)} %bitcast.16) | data formatting | bytes 1048576
  (2 shorter events, 0.1 us)
Async XLA Ops:
  0.6 1.2 %copy-start = (bf16[32,16,512]{2,1,0:T(8,128)(2,1)S(1)}, bf16[32,16,512]{2,1,0:T(8,128)(2,1)}, u32[]{:S(2)}) copy-start(bf16[32,16,512]{2,1,0:T(8,128)(2,1)} %param.10) | copy-start | bytes 1572868
  0.6 1.2 %copy-start.5 = (f32[256,128]{1,0:T(8,128)S(1)}, f32[256,128]{1,0:T(8,128)}, u32[]{:S(2)}) copy-start(f32[256,128]{1,0:T(8,128)} %constant.17.clone.refs_9_) | copy-start | bytes 393220
  1.8 1.0 %copy-start.1 = (bf16[64,8,256]{2,1,0:T(8,128)(2,1)S(1)}, bf16[64,8,256]{2,1,0:T(8,128)(2,1)}, u32[]{:S(2)}) copy-start(bf16[64,8,256]{2,1,0:T(8,128)(2,1)} %param.13) | copy-start | bytes 786436
  2.8 0.9 %copy-start.2 = (bf16[5,5,64,32]{2,3,1,0:T(8,128)(2,1)S(1)}, bf16[5,5,64,32]{2,3,1,0:T(8,128)(2,1)}, u32[]{:S(2)}) copy-start(bf16[5,5,64,32]{2,3,1,0:T(8,128)(2,1)} %param.11) | copy-start | bytes 307204
  3.7 0.9 %copy-start.3 = (bf16[2,256,256]{2,1,0:T(8,128)(2,1)S(1)}, bf16[2,256,256]{2,1,0:T(8,128)(2,1)}, u32[]{:S(2)}) copy-start(bf16[2,256,256]{2,1,0:T(8,128)(2,1)} %constant.15.clone.refs_7_) | copy-start | bytes 786436
  4.7 0.9 %copy-start.4 = (bf16[2,256,256]{2,1,0:T(8,128)(2,1)S(1)}, bf16[2,256,256]{2,1,0:T(8,128)(2,1)}, u32[]{:S(2)}) copy-start(bf16[2,256,256]{2,1,0:T(8,128)(2,1)} %constant.14.clone.refs_6_) | copy-start | bytes 786436
  5.6 0.9 %copy-start.6 = (f32[256,128]{1,0:T(8,128)S(1)}, f32[256,128]{1,0:T(8,128)}, u32[]{:S(2)}) copy-start(f32[256,128]{1,0:T(8,128)} %constant.16.clone.refs_8_) | copy-start | bytes 393220

commit v3 on v2

--- a/solution.py
+++ b/solution.py
@@ -394,7 +394,7 @@
             shape((2, chans, lanes, outer), f32),
             shape((count, 16, part_width), f32),
         ],
-        in_specs=[vmem] * 4 + [pl.BlockSpec(memory_space=pl.ANY)] * 6,
+        in_specs=[vmem] * 4 + [pl.BlockSpec(memory_space=pltpu.HBM)] * 6,
         out_specs=[vmem] * 3,
         scratch_shapes=[pltpu.VMEM(table.shape, table.dtype) for table in tables]
         + [

time: 60 us -> 60 us (level)
  no operation moved by 1% of the time
where the time goes in v3:
time: 60 us; the launch traced here: 59.7 us
  Pallas kernels  50.3 us (84%)
  local copies, waits for them, and re-layouts  8.72 us (15%)
  between operations  0.71 us (1%)
    pallas_call x1, Pallas kernels, per_device(): pl.pallas_call(body, out_shape=[shape((cin * tw, width), bf16), shape((2,...  50.3 us
    unnamed x16, local copies, waits for them, and re-layouts  5.53 us

profile of v3, /device:TPU:0, one launch (start us, length us, event | category | flops | bytes accessed | tf_op | source)
XLA Modules:
  0.0 59.7 jit_solution(6681884357909342784)
XLA Ops:
  0.6 0.0 copy-start
  0.6 0.0 copy-start.5
  0.7 1.1 %reshape.36.refs_3_ = f32[2,4,128,32]{3,2,1,0:T(8,128)S(1)} reshape(f32[2,4,4096]{2,1,0:T(4,128)} %param.12) | data formatting | bytes 262144 | tf_op jit(solution)/shard_map/reshape | solution.py:434
  1.8 0.0 copy-done
  1.8 0.0 copy-done.5
  1.8 0.0 copy-start.1
  1.8 0.9 %copy-done.1 = bf16[64,8,256]{2,1,0:T(8,128)(2,1)S(1)} copy-done((bf16[64,8,256]{2,1,0:T(8,128)(2,1)S(1)}, bf16[64,8,256]{2,1,0:T(8,128)(2,1)}, u32[]{:S(2)}) %copy-start.1) | copy-done | bytes 262168
  2.8 0.0 copy-start.2
  2.8 0.9 %copy-done.2 = bf16[5,5,64,32]{2,3,1,0:T(8,128)(2,1)S(1)} copy-done((bf16[5,5,64,32]{2,3,1,0:T(8,128)(2,1)S(1)}, bf16[5,5,64,32]{2,3,1,0:T(8,128)(2,1)}, u32[]{:S(2)}) %copy-start.2) | copy-done | bytes 102424
  3.7 0.0 copy-start.3
  3.7 0.9 %copy-done.3 = bf16[2,256,256]{2,1,0:T(8,128)(2,1)S(1)} copy-done((bf16[2,256,256]{2,1,0:T(8,128)(2,1)S(1)}, bf16[2,256,256]{2,1,0:T(8,128)(2,1)}, u32[]{:S(2)}) %copy-start.3) | copy-done | bytes 262168
  4.7 0.0 copy-start.4
  4.7 0.9 %copy-done.4 = bf16[2,256,256]{2,1,0:T(8,128)(2,1)S(1)} copy-done((bf16[2,256,256]{2,1,0:T(8,128)(2,1)S(1)}, bf16[2,256,256]{2,1,0:T(8,128)(2,1)}, u32[]{:S(2)}) %copy-start.4) | copy-done | bytes 262168
  5.6 0.0 copy-start.6
  5.6 0.9 %copy-done.6 = f32[256,128]{1,0:T(8,128)S(1)} copy-done((f32[256,128]{1,0:T(8,128)S(1)}, f32[256,128]{1,0:T(8,128)}, u32[]{:S(2)}) %copy-start.6) | copy-done | bytes 131096
  6.5 50.3 %shard_map.121 = (bf16[512,512]{1,0:T(8,128)(2,1)S(1)}, f32[2,4,128,32]{3,2,1,0:T(8,128)S(1)}, f32[16,16,256]{2,1,0:T(8,128)S(1)}) custom-call(bf16[512,512]{1,0:T(8,128)(2,1)S(1)} %bitcast.18, bf16[16,32,256]{2,1,0:T(8,128)(2,1)S(1)} %bitcast.19, bf16[800,64]{1,0:T(8,128)(2,1)S(1)} %bitcast.20, f32[2,4,128,32]{3,2,1,0:T(8,128)S(1)} %reshape.36.refs_3_, ...), custom_call_target="tpu_custom_call" | custom-call | flops 6000000000 | bytes 8000000 | tf_op jit(solution)/shard_map/pallas_call | solution.py:390
  56.8 0.2 copy.15
  57.1 0.9 %reshape.41 = f32[2,4,4096]{2,1,0:T(4,128)} reshape(f32[2,4,128,32]{3,2,1,0:T(8,128)S(1)} %get-tuple-element.8) | data formatting | bytes 262144 | tf_op jit(solution)/shard_map/reshape | solution.py:437
  58.0 0.9 %copy.16 = f32[64,800]{0,1:T(8,128)} copy(f32[64,800]{1,0:T(8,128)S(1)} %slice.4) | data formatting | bytes 409600 | tf_op jit(solution)/shard_map/slice | solution.py:439
  58.9 0.8 %copy.19 = bf16[32,16,512]{2,1,0:T(8,128)(2,1)} copy(bf16[32,16,512]{2,1,0:T(8,128)(2,1)S(1)} %bitcast.16) | data formatting | bytes 1048576
  (2 shorter events, 0.1 us)
Async XLA Ops:
  0.6 1.2 %copy-start = (bf16[32,16,512]{2,1,0:T(8,128)(2,1)S(1)}, bf16[32,16,512]{2,1,0:T(8,128)(2,1)}, u32[]{:S(2)}) copy-start(bf16[32,16,512]{2,1,0:T(8,128)(2,1)} %param.10) | copy-start | bytes 1572868
  0.6 1.2 %copy-start.5 = (f32[256,128]{1,0:T(8,128)S(1)}, f32[256,128]{1,0:T(8,128)}, u32[]{:S(2)}) copy-start(f32[256,128]{1,0:T(8,128)} %constant.17.clone.refs_9_) | copy-start | bytes 393220
  1.8 1.0 %copy-start.1 = (bf16[64,8,256]{2,1,0:T(8,128)(2,1)S(1)}, bf16[64,8,256]{2,1,0:T(8,128)(2,1)}, u32[]{:S(2)}) copy-start(bf16[64,8,256]{2,1,0:T(8,128)(2,1)} %param.13) | copy-start | bytes 786436
  2.8 0.9 %copy-start.2 = (bf16[5,5,64,32]{2,3,1,0:T(8,128)(2,1)S(1)}, bf16[5,5,64,32]{2,3,1,0:T(8,128)(2,1)}, u32[]{:S(2)}) copy-start(bf16[5,5,64,32]{2,3,1,0:T(8,128)(2,1)} %param.11) | copy-start | bytes 307204
  3.7 0.9 %copy-start.3 = (bf16[2,256,256]{2,1,0:T(8,128)(2,1)S(1)}, bf16[2,256,256]{2,1,0:T(8,128)(2,1)}, u32[]{:S(2)}) copy-start(bf16[2,256,256]{2,1,0:T(8,128)(2,1)} %constant.15.clone.refs_7_) | copy-start | bytes 786436
  4.7 0.9 %copy-start.4 = (bf16[2,256,256]{2,1,0:T(8,128)(2,1)S(1)}, bf16[2,256,256]{2,1,0:T(8,128)(2,1)}, u32[]{:S(2)}) copy-start(bf16[2,256,256]{2,1,0:T(8,128)(2,1)} %constant.14.clone.refs_6_) | copy-start | bytes 786436
  5.6 0.9 %copy-start.6 = (f32[256,128]{1,0:T(8,128)S(1)}, f32[256,128]{1,0:T(8,128)}, u32[]{:S(2)}) copy-start(f32[256,128]{1,0:T(8,128)} %constant.16.clone.refs_8_) | copy-start | bytes 393220
